TPU v7x, 256 devices: a whole 4x4x8 slice. The times are simulated.
256 devices in a mesh: row: 16 (over z_hi, x, core), col: 16 (over z_lo, y).
Axes of the slice: x: 4, y: 4, z: 8 (z_hi: 2, z_lo: 4; z = z_hi * 4 + z_lo), core: 2. Of those that a mesh axis runs over, the one named last changes fastest.
Arguments:
- tokens: bfloat16 [131072, 1024], P(('row', 'col')), may hold values from -6 to 6
- gate: bfloat16 [131072, 1024], P('row', 'col'), may hold values from -6 to 6
- filter_spectrum: float32 [2, 256, 128, 1024], P(None, None, None, ('col', 'row')), may hold values from -12 to 12
- skip_gain: float32 [1024], P(('col', 'row')), may hold values from 0.3 to 3
- kept_blocks: int32 [256], replicated, may hold values from 0 to 1023, as said below
- out_weight: bfloat16 [1024, 2048], P('col'), may hold values from -0.1875 to 0.1875
Outputs:
- mixed: bfloat16 [131072, 2048], P(('row', 'col'))
Inputs may be any that keep to these rules, and one draw needn't show every extreme that they name: `kept_blocks`: 256 distinct block numbers in no particular order; blocks 0 and 1023 are always among them.
All inputs are finite; a program needn't handle non-finite values.
Results may differ from a plain program's by a relative error of at most 0.0058.
Values may be sent and summed in bfloat16 or wider, within the bound.
A program may use at most 192 MiB of HBM per device.

v0:
```python
import functools

import jax
import jax.numpy as jnp
import numpy as np
from jax import lax
from jax.experimental import pallas as pl
from jax.experimental.pallas import tpu as pltpu
from jax.sharding import PartitionSpec as P

SEQ = 131072
BLOCK = 128
BLOCKS = 1024
KEPT = 256
DEVICES = 256
TOKENS = SEQ // DEVICES
HALF = TOKENS
WIDTH = 4
CHUNKS = 4
TILE = 16
FEATS = 2048
MESH = pl.DeviceIdType.MESH
BF16, F32 = jnp.bfloat16, jnp.float32


def split(table):
    high = table.astype(BF16)
    low = (table - high.astype(np.float64)).astype(BF16)
    return np.stack([high, low])


def tables():
    grid = np.arange(BLOCKS)
    angle = 2.0 * np.pi * (np.outer(grid, grid) % BLOCKS) / BLOCKS
    blocks = np.concatenate([split(np.cos(angle)), split(np.sin(angle))])
    offsets = np.arange(BLOCK)
    angle = 2.0 * np.pi * np.outer(offsets, grid) / SEQ
    twist = np.stack([np.cos(angle), np.sin(angle)]).astype(np.float32)
    angle = 2.0 * np.pi * (np.outer(offsets, offsets) % BLOCK) / BLOCK
    cos, sin = np.cos(angle), np.sin(angle)
    first = np.zeros((2, 2, BLOCK, BLOCK, 2))
    last = np.zeros((BLOCK, 2, 2, 2, BLOCK))
    for p in range(2):
        first[p, 0, :, :, p], first[p, 1, :, :, p] = cos, -sin
        last[:, p, p, 0, :], last[:, p, p, 1, :] = cos, -sin
    first = split(first.reshape(512, 256))
    last = split(last.reshape(256, 512))
    pack = np.zeros((32, WIDTH, CHUNKS, CHUNKS, 32, WIDTH), np.float32)
    for o in range(32):
        for c in range(WIDTH):
            for h in range(CHUNKS):
                pack[o, c, h, h, o, c] = 1.0
    pack = pack.reshape(512, 512).astype(BF16)
    rows = np.arange(256).reshape(16, WIDTH, CHUNKS)
    eye = np.eye(256, dtype=np.float32)
    fold = eye[rows.transpose(1, 2, 0).reshape(-1)]
    order = eye[rows.transpose(2, 0, 1).reshape(-1)]
    moves = np.stack([fold, fold.T, order]).astype(BF16)
    return blocks, twist, first, last, pack, moves


def dot(a, b):
    return lax.dot_general(a, b, (((1,), (0,)), ((), ())), preferred_element_type=F32)


def dot_nt(a, b):
    return lax.dot_general(a, b, (((1,), (1,)), ((), ())), preferred_element_type=F32)


def dot_tn(a, b):
    return lax.dot_general(a, b, (((0,), (0,)), ((), ())), preferred_element_type=F32)


def halves(value):
    high = value.astype(BF16)
    return high, (value - high.astype(F32)).astype(BF16)


def kept_table(kept, blocks):
    row = lax.broadcasted_iota(jnp.int32, (KEPT, KEPT), 0)
    lane = lax.broadcasted_iota(jnp.int32, (KEPT, KEPT), 1)
    column = jnp.sum(jnp.where(row == lane, kept.astype(F32), 0.0), axis=1, keepdims=True)
    lane = lax.broadcasted_iota(jnp.int32, (KEPT, BLOCKS), 1).astype(F32)
    pick = jnp.where(lane == column, 1.0, 0.0).astype(BF16)
    return [dot(pick, blocks(i)).astype(BF16) for i in range(4)]


def kernel(
    tokens, gate, filt, skip, kept, weight, blocks, twist, first, last, pack, moves,
    out,
    tok_v, filt_v, blocks_v, twist_v, first_v, last_v, pack_v, moves_v,
    sent, got, z, tab, turn, resp, back, conv, packed, returned, gate_v, gated, w_v,
    local, own, a_send, a_recv, g_send, g_recv, w_send, w_recv, b_send, b_recv,
):
    row, col = lax.axis_index("row"), lax.axis_index("col")
    zh, x, core = row // 8, lax.rem(row, 8) // 2, lax.rem(row, 2)
    zl, y = col // 4, lax.rem(col, 4)
    as_tokens, as_channels = row * 16 + col, col * 16 + row

    barrier = pltpu.get_barrier_semaphore()

    @pl.loop(1, DEVICES)
    def _(s):
        other = (lax.rem(row + s // 16, 16), lax.rem(col + lax.rem(s, 16), 16))
        pl.semaphore_signal(barrier, inc=1, device_id=other, device_id_type=MESH)

    loads = [
        pltpu.make_async_copy(src, dst, local.at[i])
        for i, (src, dst) in enumerate(
            [(tokens, tok_v), (pack, pack_v), (blocks, blocks_v), (moves, moves_v), (first, first_v),
             (twist, twist_v), (filt, filt_v), (last, last_v)]
        )
    ]
    for load in loads:
        load.start()
    slice_at = pl.ds(pl.multiple_of((core * 4 + x) * 256, 256), 256)
    own_weight = pltpu.make_async_copy(weight.at[:, slice_at], w_v.at[zl, y, :, slice_at], own.at[0])
    own_weight.start()

    loads[0].wait()
    loads[1].wait()

    @pl.loop(0, 8)
    def _(g):
        at = pl.ds(pl.multiple_of(g * 128, 128), 128)
        wide = jnp.concatenate([tok_v[pl.ds(h * 128, 128), at] for h in range(CHUNKS)], axis=1)
        sent[pl.ds(pl.multiple_of(g * 512, 512), 512), :] = dot_nt(pack_v[...], wide).astype(BF16)

    pl.semaphore_wait(barrier, DEVICES - 1)

    def tile(index):
        return pl.ds(pl.multiple_of(index * TILE, TILE), TILE)

    def weight_copy(stage, src, dst, device):
        return pltpu.make_async_remote_copy(
            src_ref=src, dst_ref=dst, send_sem=w_send.at[stage], recv_sem=w_recv.at[stage],
            device_id=device, device_id_type=MESH,
        )

    for s in range(1, 4):
        weight_copy(
            0, weight.at[:, slice_at], w_v.at[zl, y, :, slice_at], (row, lax.rem(zl + s, 4) * 4 + y)
        ).start()

    own_tile = pltpu.make_async_copy(sent.at[tile(as_channels)], got.at[tile(as_tokens)], a_recv)
    own_tile.start()

    @pl.loop(1, DEVICES)
    def _(s):
        to_row, to_col = lax.rem(row + s // 16, 16), lax.rem(col + lax.rem(s, 16), 16)
        pltpu.make_async_remote_copy(
            src_ref=sent.at[tile(to_col * 16 + to_row)], dst_ref=got.at[tile(as_tokens)],
            send_sem=a_send, recv_sem=a_recv, device_id=(to_row, to_col), device_id_type=MESH,
        ).start()

    for load in loads[2:]:
        load.wait()
    cos_high, cos_low, sin_high, sin_low = kept_table(kept[...], lambda i: blocks_v[i])
    tab[0, 0:KEPT, :] = cos_high
    tab[0, KEPT:, :] = sin_high
    tab[1, 0:KEPT, :] = cos_low
    tab[1, KEPT:, :] = sin_low

    def weight_wait(sem, stage, ref):
        pltpu.make_async_copy(ref, ref, sem.at[stage]).wait()

    own_weight.wait()
    weight_wait(w_recv, 0, w_v.at[pl.ds(0, 3), 0, :, pl.ds(0, 256)])
    for s in range(1, 4):
        part = w_v.at[:, y, :, slice_at]
        weight_copy(1, part, part, (row, zl * 4 + lax.rem(y + s, 4))).start()

    pltpu.make_async_copy(got, got, a_recv).wait()

    own_gate = pltpu.make_async_copy(
        gate.at[:, pl.ds(pl.multiple_of(col * TOKENS, TOKENS), TOKENS)], gate_v.at[col], g_recv
    )
    own_gate.start()

    @pl.loop(1, 16)
    def _(s):
        to_col = lax.rem(col + s, 16)
        pltpu.make_async_remote_copy(
            src_ref=gate.at[:, pl.ds(pl.multiple_of(to_col * TOKENS, TOKENS), TOKENS)],
            dst_ref=gate_v.at[col], send_sem=g_send, recv_sem=g_recv,
            device_id=(row, to_col), device_id_type=MESH,
        ).start()

    weight_wait(w_recv, 1, w_v.at[:, pl.ds(0, 3), :, pl.ds(0, 256)])
    for s in range(1, 4):
        part = w_v.at[:, :, :, slice_at]
        weight_copy(2, part, part, (zh * 8 + lax.rem(x + s, 4) * 2 + core, col)).start()

    @pl.loop(0, 16)
    def _(g):
        rows = dot(moves_v[0], got[pl.ds(pl.multiple_of(g * 256, 256), 256), :]).astype(BF16)
        for c in range(WIDTH):
            for h in range(CHUNKS):
                z[c, tile(g), pl.ds(h * 128, 128)] = rows[(c * 4 + h) * 16 : (c * 4 + h) * 16 + 16, :]

    @pl.loop(0, WIDTH)
    def _(c):
        signal = z[c]
        spread = dot(first_v[0], signal) + dot(first_v[1], signal)
        for p in range(2):
            at = pl.ds(p * HALF, HALF)
            re, im = spread[p * 256 : p * 256 + 128], spread[p * 256 + 128 : p * 256 + 256]
            cos, sin = twist_v[0, :, at], twist_v[1, :, at]
            turn[0, 0:128, at], turn[1, 0:128, at] = halves(re * cos + im * sin)
            turn[0, 128:256, at], turn[1, 128:256, at] = halves(im * cos - re * sin)
        spec = dot_nt(tab[0], turn[0]) + dot_nt(tab[1], turn[0]) + dot_nt(tab[0], turn[1])
        spec_re = spec[:KEPT, :128] + spec[KEPT:, 128:]
        spec_im = spec[:KEPT, 128:] - spec[KEPT:, :128]
        filt_re, filt_im = filt_v[0, c], filt_v[1, c]
        re = halves(filt_re * spec_re - filt_im * spec_im)
        im = halves(filt_re * spec_im + filt_im * spec_re)
        for i in range(2):
            resp[i, 0:KEPT, 0:128] = re[i]
            resp[i, 0:KEPT, 128:256] = im[i]
            resp[i, KEPT:, 0:128] = -im[i]
            resp[i, KEPT:, 128:256] = re[i]
        wave = dot_tn(resp[0], tab[0]) + dot_tn(resp[1], tab[0]) + dot_tn(resp[0], tab[1])
        for p in range(2):
            at = pl.ds(p * HALF, HALF)
            re, im = wave[:128, p * HALF : p * HALF + HALF], wave[128:, p * HALF : p * HALF + HALF]
            cos, sin = twist_v[0, :, at], twist_v[1, :, at]
            at = p * 256
            back[0, at : at + 128, :], back[1, at : at + 128, :] = halves(re * cos - im * sin)
            back[0, at + 128 : at + 256, :], back[1, at + 128 : at + 256, :] = halves(im * cos + re * sin)
        result = dot(last_v[0], back[0]) + dot(last_v[1], back[0]) + dot(last_v[0], back[1])
        conv[c] = (result * (1.0 / SEQ) + skip[c] * signal.astype(F32)).astype(BF16)

    @pl.loop(0, 16)
    def _(g):
        rows = jnp.concatenate(
            [conv[c, tile(g), pl.ds(h * 128, 128)] for c in range(WIDTH) for h in range(CHUNKS)], axis=0
        )
        packed[pl.ds(pl.multiple_of(g * 256, 256), 256), :] = dot(moves_v[1], rows).astype(BF16)

    own_back = pltpu.make_async_copy(packed.at[tile(as_tokens)], returned.at[tile(as_channels)], b_recv)
    own_back.start()

    @pl.loop(1, DEVICES)
    def _(s):
        to_row, to_col = lax.rem(row + s // 16, 16), lax.rem(col + lax.rem(s, 16), 16)
        pltpu.make_async_remote_copy(
            src_ref=packed.at[tile(to_row * 16 + to_col)], dst_ref=returned.at[tile(as_channels)],
            send_sem=b_send, recv_sem=b_recv, device_id=(to_row, to_col), device_id_type=MESH,
        ).start()

    weight_wait(w_recv, 2, w_v.at[:, :, :, pl.ds(0, 768)])
    half = w_v.at[:, :, :, pl.ds(pl.multiple_of(core * 1024, 1024), 1024)]
    weight_copy(3, half, half, (row + 1 - 2 * core, col)).start()

    pltpu.make_async_copy(gate_v, gate_v, g_recv).wait()
    weight_wait(w_recv, 3, w_v.at[:, :, :, pl.ds(0, 1024)])
    pltpu.make_async_copy(returned, returned, b_recv).wait()

    @pl.loop(0, 16)
    def _(g):
        rows = dot(moves_v[2], returned[pl.ds(pl.multiple_of(g * 256, 256), 256), :])
        for h in range(CHUNKS):
            at = pl.ds(h * 128, 128)
            piece = rows[h * 64 : h * 64 + 64] * gate_v[g, :, at].astype(F32)
            gated[pl.ds(pl.multiple_of(g * 64, 64), 64), at] = piece.astype(BF16)

    @pl.loop(0, 4)
    def _(n):
        at = pl.ds(pl.multiple_of(n * 512, 512), 512)
        out[:, at] = dot_tn(gated[...], w_v[:, :, :, at].reshape(1024, 512)).astype(BF16)

    pltpu.make_async_copy(sent.at[pl.ds(0, 4080)], sent.at[pl.ds(0, 4080)], a_send).wait()
    pltpu.make_async_copy(packed.at[pl.ds(0, 4080)], packed.at[pl.ds(0, 4080)], b_send).wait()
    pltpu.make_async_copy(gate_v.at[pl.ds(0, 15)], gate_v.at[pl.ds(0, 15)], g_send).wait()
    weight_wait(w_send, 0, w_v.at[pl.ds(0, 3), 0, :, pl.ds(0, 256)])
    weight_wait(w_send, 1, w_v.at[:, pl.ds(0, 3), :, pl.ds(0, 256)])
    weight_wait(w_send, 2, w_v.at[:, :, :, pl.ds(0, 768)])
    weight_wait(w_send, 3, w_v.at[:, :, :, pl.ds(0, 1024)])


def on_device(tokens, gate, filter_spectrum, skip_gain, kept_blocks, out_weight):
    blocks, twist, first, last, pack, moves = (jnp.asarray(t) for t in tables())
    filt = jnp.transpose(filter_spectrum, (0, 3, 1, 2))
    hbm = pl.BlockSpec(memory_space=pl.ANY)
    vmem = pl.BlockSpec(memory_space=pltpu.VMEM)
    smem = pl.BlockSpec(memory_space=pltpu.SMEM)
    like = lambda t: pltpu.VMEM(t.shape, t.dtype)
    return pl.pallas_call(
        kernel,
        out_shape=jax.ShapeDtypeStruct((TOKENS, FEATS), BF16),
        in_specs=[hbm, hbm, hbm, smem, vmem, hbm, hbm, hbm, hbm, hbm, hbm, hbm],
        out_specs=vmem,
        scratch_shapes=[
            like(tokens), like(filt), like(blocks), like(twist), like(first), like(last), like(pack), like(moves),
            pltpu.VMEM((4096, 128), BF16),
            pltpu.VMEM((4096, 128), BF16),
            pltpu.VMEM((WIDTH, 256, 512), BF16),
            pltpu.VMEM((2, 2 * KEPT, BLOCKS), BF16),
            pltpu.VMEM((2, 256, BLOCKS), BF16),
            pltpu.VMEM((2, 2 * KEPT, 256), BF16),
            pltpu.VMEM((2, 512, 512), BF16),
            pltpu.VMEM((WIDTH, 256, 512), BF16),
            pltpu.VMEM((4096, 128), BF16),
            pltpu.VMEM((4096, 128), BF16),
            pltpu.VMEM((16, 64, TOKENS), BF16),
            pltpu.VMEM((1024, TOKENS), BF16),
            pltpu.VMEM((4, 4, 64, FEATS), BF16),
            pltpu.SemaphoreType.DMA((8,)),
            pltpu.SemaphoreType.DMA((1,)),
            pltpu.SemaphoreType.DMA,
            pltpu.SemaphoreType.DMA,
            pltpu.SemaphoreType.DMA,
            pltpu.SemaphoreType.DMA,
            pltpu.SemaphoreType.DMA((4,)),
            pltpu.SemaphoreType.DMA((4,)),
            pltpu.SemaphoreType.DMA,
            pltpu.SemaphoreType.DMA,
        ],
        compiler_params=pltpu.CompilerParams(
            collective_id=0, has_side_effects=True, vmem_limit_bytes=56 * 1024 * 1024
        ),
    )(tokens, gate.T, filt, skip_gain, kept_blocks.reshape(1, KEPT), out_weight, blocks, twist, first, last, pack, moves)


def solution(mesh):
    return jax.shard_map(
        on_device,
        mesh=mesh,
        in_specs=(
            P(("row", "col"), None),
            P("row", "col"),
            P(None, None, None, ("col", "row")),
            P(("col", "row")),
            P(),
            P("col", None),
        ),
        out_specs=P(("row", "col"), None),
        check_vma=False,
    )
```

profile of v0, /device:TPU:1, one launch (start us, length us, event | category | flops | bytes accessed | tf_op | source)
XLA Modules:
  0.0 109.9 jit_solution(16078072278966171124)
XLA Ops:
  0.0 2.3 %copy.15 = f32[2,256,128,4]{2,1,3,0:T(8,128)} copy(f32[2,256,128,4]{2,3,1,0:T(4,128)} %param.14) | data formatting | bytes 2097152 | tf_op args[2]
  2.3 104.4 %shard_map.118 = bf16[512,2048]{1,0:T(8,128)(2,1)} custom-call(bf16[512,1024]{1,0:T(8,128)(2,1)} %tokens.1, bf16[64,8192]{1,0:T(8,128)(2,1)} %bitcast.6, f32[2,4,256,128]{3,2,1,0:T(8,128)} %bitcast.5, f32[4]{0:T(128)} %skip.1, s32[1,256]{1,0:T(1,128)} %bitcast.7, bf16[64,2048]{1,0:T(8,128)(2,1)} %weight.1, bf16[4,1024,1024]{2,1,0:T(8,128)(2,1)} %constant.12.clone.blocks, ...), custom_call_target="tpu_custom_call" | custom-call | tf_op jit(solution)/shard_map/pallas_call | solution.py:288
  106.7 3.2 %copy.17 = bf16[512,2048]{1,0:T(8,128)(2,1)} copy(bf16[512,2048]{1,0:T(8,128)(2,1)} %shard_map.118) | data formatting | bytes 4194304
where the time goes:
time: 110 us
  Pallas kernels  104 us (95%)
  local copies, waits for them, and re-layouts  5.44 us (5%)
    pallas_call x1, Pallas kernels, on_device(): pl.pallas_call(kernel, out_shape=jax.ShapeDtypeStruct((TOKENS, FEATS), BF...  104 us
    unnamed x2, local copies, waits for them, and re-layouts  5.44 us

commit v1 on v0

v1 whole, which is shorter than its diff:
```python
import functools

import jax
import jax.numpy as jnp
import numpy as np
from jax import lax
from jax.experimental import pallas as pl
from jax.experimental.pallas import tpu as pltpu
from jax.sharding import PartitionSpec as P

SEQ = 131072
BLOCK = 128
BLOCKS = 1024
KEPT = 256
DEVICES = 256
TOKENS = SEQ // DEVICES
PAIRS = BLOCK // 2
WIDTH = 4
CHUNKS = 4
TILE = 16
FEATS = 2048
MESH = pl.DeviceIdType.MESH
BF16, F32 = jnp.bfloat16, jnp.float32


def split(table):
    high = table.astype(BF16)
    low = (table - high.astype(np.float64)).astype(BF16)
    return np.stack([high, low])


def tables():
    grid = np.arange(BLOCKS)
    angle = 2.0 * np.pi * (np.outer(2 * grid + 1, grid) % (2 * BLOCKS)) / (2 * BLOCKS)
    blocks = np.concatenate([split(np.cos(angle)), split(np.sin(angle))])
    pairs = np.arange(PAIRS)
    angle = 2.0 * np.pi * np.outer(pairs, grid) / SEQ
    cos, sin = np.cos(angle), np.sin(angle)
    masked = cos.copy()
    masked[0] = 0.0
    twist = np.stack([cos, sin, masked]).astype(np.float32)
    angle = 2.0 * np.pi * PAIRS * grid / SEQ
    edge = np.stack([np.cos(angle), np.sin(angle)]).astype(np.float32)
    j = np.arange(BLOCK)
    sign = (-1.0) ** j
    angle = 2.0 * np.pi * (np.outer(pairs, j) % BLOCK) / BLOCK
    real, imag = sign * np.cos(angle), -sign * np.sin(angle)
    imag[0] = 1.0
    first = np.zeros((2, 2, PAIRS, BLOCK, 2))
    for p in range(2):
        first[p, 0, :, :, p], first[p, 1, :, :, p] = real, imag
    first = first.reshape(256, 256)
    last = split(first.T.copy())
    first = split(first)
    pack = np.zeros((32, WIDTH, CHUNKS, CHUNKS, 32, WIDTH), np.float32)
    for o in range(32):
        for c in range(WIDTH):
            for h in range(CHUNKS):
                pack[o, c, h, h, o, c] = 1.0
    pack = pack.reshape(512, 512).astype(BF16)
    rows = np.arange(256).reshape(16, WIDTH, CHUNKS)
    eye = np.eye(256, dtype=np.float32)
    fold = eye[rows.transpose(1, 2, 0).reshape(-1)]
    rows = rows.reshape(2, 8, WIDTH, CHUNKS)
    order = eye[rows.transpose(0, 3, 1, 2).reshape(-1)]
    moves = np.stack([fold, fold.T, order]).astype(BF16)
    offsets = np.concatenate([64 + pairs, [0], 64 - pairs[1:]])
    mirror = np.eye(BLOCK, dtype=np.float32)[offsets].astype(BF16)
    return blocks, twist, edge, first, last, pack, moves, mirror


def dot(a, b):
    return lax.dot_general(a, b, (((1,), (0,)), ((), ())), preferred_element_type=F32)


def dot_nt(a, b):
    return lax.dot_general(a, b, (((1,), (1,)), ((), ())), preferred_element_type=F32)


def dot_tn(a, b):
    return lax.dot_general(a, b, (((0,), (0,)), ((), ())), preferred_element_type=F32)


def halves(value):
    high = value.astype(BF16)
    return high, (value - high.astype(F32)).astype(BF16)


def kept_table(kept, blocks):
    row = lax.broadcasted_iota(jnp.int32, (KEPT, KEPT), 0)
    lane = lax.broadcasted_iota(jnp.int32, (KEPT, KEPT), 1)
    column = jnp.sum(jnp.where(row == lane, kept.astype(F32), 0.0), axis=1, keepdims=True)
    lane = lax.broadcasted_iota(jnp.int32, (KEPT, BLOCKS), 1).astype(F32)
    pick = jnp.where(lane == column, 1.0, 0.0).astype(BF16)
    return [dot(pick, blocks[i]).astype(BF16) for i in range(4)]


def prepare(kept, blocks_v, filt_v, mirror_v, tab, filt_p):
    cos_high, cos_low, sin_high, sin_low = kept_table(kept[...], blocks_v)
    tab[0, 0:KEPT, :] = cos_high
    tab[0, KEPT:, :] = sin_high
    tab[1, 0:KEPT, :] = cos_low
    tab[1, KEPT:, :] = sin_low
    for i in range(2):
        for c in range(WIDTH):
            high, low = halves(filt_v[i, c])
            filt_p[i, c] = dot_nt(mirror_v[...], high) + dot_nt(mirror_v[...], low)


def convolve(z, first_v, last_v, twist_v, edge_v, tab, filt_p, skip, ends, turn, spec, resp, wave, back, conv):
    @pl.loop(0, WIDTH)
    def _(c):
        signal = z[c]
        spread = dot(first_v[0], signal) + dot(first_v[1], signal)
        rows = pl.ds(pl.multiple_of(c * 128, 128), 128)
        for p in range(2):
            at = pl.ds(p * TOKENS, TOKENS)
            re, im = spread[p * 128 : p * 128 + 64], spread[p * 128 + 64 : p * 128 + 128]
            cos, sin, masked = twist_v[0, :, at], twist_v[1, :, at], twist_v[2, :, at]
            both = jnp.concatenate([re * cos + im * sin, im * masked - re * sin], axis=0)
            turn[0, rows, at], turn[1, rows, at] = halves(both)
            ends[pl.ds(c, 1), at] = im[0:1]

    edge = ends[0:4, :]
    both = [edge * edge_v[0:1, :], edge * -edge_v[1:2, :], jnp.zeros((8, BLOCKS), F32)]
    turn[0, 512:528, :], turn[1, 512:528, :] = halves(jnp.concatenate(both, axis=0))

    spec[...] = dot_nt(turn[0], tab[0]) + dot_nt(turn[1], tab[0]) + dot_nt(turn[0], tab[1])

    top = lax.broadcasted_iota(jnp.int32, (PAIRS, KEPT), 0) == 0
    ends_re, ends_im = [], []
    for c in range(WIDTH):
        at = c * 128
        cos_re, sin_re = spec[at : at + 64, :KEPT], spec[at : at + 64, KEPT:]
        cos_im, sin_im = spec[at + 64 : at + 128, :KEPT], spec[at + 64 : at + 128, KEPT:]
        up_re, up_im = cos_re + sin_im, cos_im - sin_re
        edge_re = spec[512 + c : 513 + c, :KEPT] - spec[516 + c : 517 + c, KEPT:]
        edge_im = -spec[516 + c : 517 + c, :KEPT] - spec[512 + c : 513 + c, KEPT:]
        down_re = jnp.where(top, edge_re, cos_re - sin_im)
        down_im = jnp.where(top, edge_im, -cos_im - sin_re)
        filt_re, filt_im = filt_p[0, c, 0:64], filt_p[1, c, 0:64]
        up_re, up_im = filt_re * up_re - filt_im * up_im, filt_re * up_im + filt_im * up_re
        filt_re, filt_im = filt_p[0, c, 64:128], filt_p[1, c, 64:128]
        down_re, down_im = filt_re * down_re - filt_im * down_im, filt_re * down_im + filt_im * down_re
        ends_re.append(jnp.concatenate([down_re[0:1], -down_im[0:1]], axis=1))
        ends_im.append(jnp.concatenate([-down_im[0:1], -down_re[0:1]], axis=1))
        down_re, down_im = jnp.where(top, 0.0, down_re), jnp.where(top, 0.0, down_im)
        both = jnp.concatenate(
            [
                jnp.concatenate([up_re + down_re, -(up_im + down_im)], axis=1),
                jnp.concatenate([up_im - down_im, up_re - down_re], axis=1),
            ],
            axis=0,
        )
        resp[0, at : at + 128, :], resp[1, at : at + 128, :] = halves(both)
    both = jnp.concatenate(ends_re + ends_im + [jnp.zeros((8, 2 * KEPT), F32)], axis=0)
    resp[0, 512:528, :], resp[1, 512:528, :] = halves(both)

    wave[...] = dot(resp[0], tab[0]) + dot(resp[1], tab[0]) + dot(resp[0], tab[1])
    edge = wave[512:516, :] * edge_v[0:1, :] - wave[516:520, :] * edge_v[1:2, :]
    ends[0:4, :] = edge

    @pl.loop(0, WIDTH)
    def _(c):
        top = lax.broadcasted_iota(jnp.int32, (PAIRS, TOKENS), 0) == 0
        start = pl.multiple_of(c * 128, 128)
        for p in range(2):
            at = pl.ds(p * TOKENS, TOKENS)
            re, im = wave[pl.ds(start, 64), at], wave[pl.ds(start + 64, 64), at]
            cos, sin = twist_v[0, :, at], twist_v[1, :, at]
            low = jnp.where(top, ends[pl.ds(c, 1), at], im * cos + re * sin)
            both = jnp.concatenate([re * cos - im * sin, low], axis=0)
            back[0, p * 128 : p * 128 + 128, :], back[1, p * 128 : p * 128 + 128, :] = halves(both)
        result = dot(last_v[0], back[0]) + dot(last_v[1], back[0]) + dot(last_v[0], back[1])
        conv[c] = (result * (1.0 / SEQ) + skip[c] * z[c].astype(F32)).astype(BF16)


def kernel(
    tokens, gate, filt, skip, kept, weight, blocks, twist, edge, first, last, pack, moves, mirror,
    out,
    tok_v, filt_v, blocks_v, twist_v, edge_v, first_v, last_v, pack_v, moves_v, mirror_v,
    sent, got, z, tab, filt_p, ends, turn, spec, resp, wave, back, conv, packed, returned, near, near_gate, near_out,
    gate_v, gated, w_v,
    local, own, a_send, a_recv, g_send, g_recv, w_send, w_recv, b_send, b_recv, n_send, n_recv, m_send, m_recv,
):
    row, col = lax.axis_index("row"), lax.axis_index("col")
    zh, x, core = row // 8, lax.rem(row, 8) // 2, lax.rem(row, 2)
    low_row = lax.rem(row, 8)
    zl, y = col // 4, lax.rem(col, 4)
    as_tokens, as_channels = row * 16 + col, col * 16 + row

    barrier = pltpu.get_barrier_semaphore()

    @pl.loop(1, DEVICES)
    def _(s):
        other = (lax.rem(row + s // 16, 16), lax.rem(col + lax.rem(s, 16), 16))
        pl.semaphore_signal(barrier, inc=1, device_id=other, device_id_type=MESH)

    same = pl.multiple_of(zh * 32, 32)
    cross = pl.multiple_of(32 - zh * 32, 32)
    loads = [
        pltpu.make_async_copy(src, dst, local.at[i])
        for i, (src, dst) in enumerate(
            [(tokens, tok_v), (pack, pack_v), (blocks, blocks_v), (moves, moves_v), (first, first_v),
             (twist, twist_v), (last, last_v), (edge, edge_v), (mirror, mirror_v),
             (gate.at[pl.ds(same, 32), :], near_gate), (filt, filt_v)]
        )
    ]
    for load in loads:
        load.start()
    slice_at = pl.ds(pl.multiple_of((core * 4 + x) * 256, 256), 256)
    own_weight = pltpu.make_async_copy(weight.at[:, slice_at], w_v.at[zl, y, :, slice_at], own.at[0])
    own_weight.start()

    loads[0].wait()
    loads[1].wait()

    @pl.loop(0, 8)
    def _(g):
        at = pl.ds(pl.multiple_of(g * 128, 128), 128)
        wide = jnp.concatenate([tok_v[pl.ds(h * 128, 128), at] for h in range(CHUNKS)], axis=1)
        sent[pl.ds(pl.multiple_of(g * 512, 512), 512), :] = dot_nt(pack_v[...], wide).astype(BF16)

    pl.semaphore_wait(barrier, DEVICES - 1)

    def tile(index):
        return pl.ds(pl.multiple_of(index * TILE, TILE), TILE)

    def weight_copy(stage, src, dst, device):
        return pltpu.make_async_remote_copy(
            src_ref=src, dst_ref=dst, send_sem=w_send.at[stage], recv_sem=w_recv.at[stage],
            device_id=device, device_id_type=MESH,
        )

    own_tile = pltpu.make_async_copy(sent.at[tile(as_channels)], got.at[tile(as_tokens)], a_recv)
    own_tile.start()

    @pl.loop(1, DEVICES)
    def _(s):
        to_row, to_col = lax.rem(row + s // 16, 16), lax.rem(col + lax.rem(s, 16), 16)
        pltpu.make_async_remote_copy(
            src_ref=sent.at[tile(to_col * 16 + to_row)], dst_ref=got.at[tile(as_tokens)],
            send_sem=a_send, recv_sem=a_recv, device_id=(to_row, to_col), device_id_type=MESH,
        ).start()

    for s in range(1, 4):
        weight_copy(
            0, weight.at[:, slice_at], w_v.at[zl, y, :, slice_at], (row, lax.rem(zl + s, 4) * 4 + y)
        ).start()

    for load in loads[2:]:
        load.wait()
    prepare(kept, blocks_v, filt_v, mirror_v, tab, filt_p)

    def weight_wait(sem, stage, ref):
        pltpu.make_async_copy(ref, ref, sem.at[stage]).wait()

    own_weight.wait()
    weight_wait(w_recv, 0, w_v.at[pl.ds(0, 3), 0, :, pl.ds(0, 256)])
    for s in range(1, 4):
        part = w_v.at[:, y, :, slice_at]
        weight_copy(1, part, part, (row, zl * 4 + lax.rem(y + s, 4))).start()

    pltpu.make_async_copy(got, got, a_recv).wait()

    def gate_at(to_col):
        return gate.at[pl.ds(cross, 32), pl.ds(pl.multiple_of(to_col * TOKENS, TOKENS), TOKENS)]

    own_gate = pltpu.make_async_copy(gate_at(col), gate_v.at[col], g_recv)
    own_gate.start()

    @pl.loop(1, 16)
    def _(s):
        to_col = lax.rem(col + s, 16)
        pltpu.make_async_remote_copy(
            src_ref=gate_at(to_col), dst_ref=gate_v.at[col], send_sem=g_send, recv_sem=g_recv,
            device_id=(row, to_col), device_id_type=MESH,
        ).start()

    weight_wait(w_recv, 1, w_v.at[:, pl.ds(0, 3), :, pl.ds(0, 256)])
    for s in range(1, 4):
        part = w_v.at[:, :, :, slice_at]
        weight_copy(2, part, part, (zh * 8 + lax.rem(x + s, 4) * 2 + core, col)).start()

    @pl.loop(0, 16)
    def _(g):
        rows = dot(moves_v[0], got[pl.ds(pl.multiple_of(g * 256, 256), 256), :]).astype(BF16)
        for c in range(WIDTH):
            for h in range(CHUNKS):
                z[c, tile(g), pl.ds(h * 128, 128)] = rows[(c * 4 + h) * 16 : (c * 4 + h) * 16 + 16, :]

    convolve(z, first_v, last_v, twist_v, edge_v, tab, filt_p, skip, ends, turn, spec, resp, wave, back, conv)

    @pl.loop(0, 16)
    def _(g):
        rows = jnp.concatenate(
            [conv[c, tile(g), pl.ds(h * 128, 128)] for c in range(WIDTH) for h in range(CHUNKS)], axis=0
        )
        packed[pl.ds(pl.multiple_of(g * 256, 256), 256), :] = dot(moves_v[1], rows).astype(BF16)

    def row_tiles(index):
        return pl.ds(pl.multiple_of(index * 256, 256), 256)

    own_near = pltpu.make_async_copy(packed.at[row_tiles(row)], near.at[row_tiles(low_row)], n_recv)
    own_near.start()

    @pl.loop(1, 8)
    def _(s):
        to_row = zh * 8 + lax.rem(low_row + s, 8)
        pltpu.make_async_remote_copy(
            src_ref=packed.at[row_tiles(to_row)], dst_ref=near.at[row_tiles(low_row)],
            send_sem=n_send, recv_sem=n_recv, device_id=(to_row, col), device_id_type=MESH,
        ).start()

    @pl.loop(0, 128)
    def _(s):
        to_row = (1 - zh) * 8 + lax.rem(low_row + s // 16, 8)
        to_col = lax.rem(col + lax.rem(s, 16), 16)
        pltpu.make_async_remote_copy(
            src_ref=packed.at[tile(to_row * 16 + to_col)], dst_ref=returned.at[tile(col * 8 + low_row)],
            send_sem=b_send, recv_sem=b_recv, device_id=(to_row, to_col), device_id_type=MESH,
        ).start()

    pltpu.make_async_copy(near, near, n_recv).wait()

    @pl.loop(0, 8)
    def _(g):
        rows = jnp.concatenate([near[tile(s * 16 + g * 2 + i), :] for i in range(2) for s in range(8)], axis=0)
        rows = dot(moves_v[2], rows)
        for i in range(2):
            for h in range(CHUNKS):
                at = pl.ds(pl.multiple_of((g * 2 + i) * TOKENS + h * 128, 128), 128)
                piece = rows[i * 128 + h * 32 : i * 128 + h * 32 + 32] * near_gate[:, at].astype(F32)
                near_out[g * 2 + i, :, pl.ds(h * 128, 128)] = piece.astype(BF16)

    mine = gated.at[col, pl.ds(same, 32), :]
    own_out = pltpu.make_async_copy(near_out.at[col], mine, m_recv)
    own_out.start()

    @pl.loop(1, 16)
    def _(s):
        to_col = lax.rem(col + s, 16)
        pltpu.make_async_remote_copy(
            src_ref=near_out.at[to_col], dst_ref=mine, send_sem=m_send, recv_sem=m_recv,
            device_id=(row, to_col), device_id_type=MESH,
        ).start()

    weight_wait(w_recv, 2, w_v.at[:, :, :, pl.ds(0, 768)])
    half = w_v.at[:, :, :, pl.ds(pl.multiple_of(core * 1024, 1024), 1024)]
    weight_copy(3, half, half, (row + 1 - 2 * core, col)).start()

    pltpu.make_async_copy(gate_v, gate_v, g_recv).wait()
    pltpu.make_async_copy(returned, returned, b_recv).wait()

    @pl.loop(0, 8)
    def _(g):
        rows = dot(moves_v[2], returned[pl.ds(pl.multiple_of(g * 256, 256), 256), :])
        for i in range(2):
            for h in range(CHUNKS):
                at = pl.ds(h * 128, 128)
                piece = rows[i * 128 + h * 32 : i * 128 + h * 32 + 32] * gate_v[g * 2 + i, :, at].astype(F32)
                gated[g * 2 + i, pl.ds(cross, 32), at] = piece.astype(BF16)

    weight_wait(w_recv, 3, w_v.at[:, :, :, pl.ds(0, 1024)])
    pltpu.make_async_copy(near_out, near_out, m_recv).wait()

    @pl.loop(0, 4)
    def _(n):
        at = pl.ds(pl.multiple_of(n * 512, 512), 512)
        left = gated[...].reshape(1024, TOKENS)
        out[:, at] = dot_tn(left, w_v[:, :, :, at].reshape(1024, 512)).astype(BF16)

    pltpu.make_async_copy(sent.at[pl.ds(0, 4080)], sent.at[pl.ds(0, 4080)], a_send).wait()
    pltpu.make_async_copy(returned, returned, b_send).wait()
    pltpu.make_async_copy(gate_v.at[pl.ds(0, 15)], gate_v.at[pl.ds(0, 15)], g_send).wait()
    pltpu.make_async_copy(near.at[pl.ds(0, 1792)], near.at[pl.ds(0, 1792)], n_send).wait()
    pltpu.make_async_copy(near_out.at[pl.ds(0, 15)], near_out.at[pl.ds(0, 15)], m_send).wait()
    weight_wait(w_send, 0, w_v.at[pl.ds(0, 3), 0, :, pl.ds(0, 256)])
    weight_wait(w_send, 1, w_v.at[:, pl.ds(0, 3), :, pl.ds(0, 256)])
    weight_wait(w_send, 2, w_v.at[:, :, :, pl.ds(0, 768)])
    weight_wait(w_send, 3, w_v.at[:, :, :, pl.ds(0, 1024)])


def on_device(tokens, gate, filter_spectrum, skip_gain, kept_blocks, out_weight):
    constants = [jnp.asarray(t) for t in tables()]
    filt = jnp.transpose(filter_spectrum, (0, 3, 1, 2))
    hbm = pl.BlockSpec(memory_space=pl.ANY)
    vmem = pl.BlockSpec(memory_space=pltpu.VMEM)
    smem = pl.BlockSpec(memory_space=pltpu.SMEM)
    like = lambda t: pltpu.VMEM(t.shape, t.dtype)
    dma = pltpu.SemaphoreType.DMA
    blocks, twist, edge, first, last, pack, moves, mirror = constants
    return pl.pallas_call(
        kernel,
        out_shape=jax.ShapeDtypeStruct((TOKENS, FEATS), BF16),
        in_specs=[hbm, hbm, hbm, smem, vmem, hbm] + [hbm] * 8,
        out_specs=vmem,
        scratch_shapes=[
            like(tokens), like(filt), like(blocks), like(twist), like(edge), like(first), like(last), like(pack),
            like(moves), like(mirror),
            pltpu.VMEM((4096, 128), BF16),
            pltpu.VMEM((4096, 128), BF16),
            pltpu.VMEM((WIDTH, 256, TOKENS), BF16),
            pltpu.VMEM((2, 2 * KEPT, BLOCKS), BF16),
            pltpu.VMEM((2, WIDTH, BLOCK, KEPT), F32),
            pltpu.VMEM((8, BLOCKS), F32),
            pltpu.VMEM((2, 528, BLOCKS), BF16),
            pltpu.VMEM((528, 2 * KEPT), F32),
            pltpu.VMEM((2, 528, 2 * KEPT), BF16),
            pltpu.VMEM((528, BLOCKS), F32),
            pltpu.VMEM((2, 256, TOKENS), BF16),
            pltpu.VMEM((WIDTH, 256, TOKENS), BF16),
            pltpu.VMEM((4096, 128), BF16),
            pltpu.VMEM((2048, 128), BF16),
            pltpu.VMEM((2048, 128), BF16),
            pltpu.VMEM((32, 16 * TOKENS), BF16),
            pltpu.VMEM((16, 32, TOKENS), BF16),
            pltpu.VMEM((16, 32, TOKENS), BF16),
            pltpu.VMEM((16, 64, TOKENS), BF16),
            pltpu.VMEM((4, 4, 64, FEATS), BF16),
            dma((11,)), dma((1,)), dma, dma, dma, dma, dma((4,)), dma((4,)), dma, dma, dma, dma, dma, dma,
        ],
        compiler_params=pltpu.CompilerParams(
            collective_id=0, has_side_effects=True, vmem_limit_bytes=56 * 1024 * 1024
        ),
    )(tokens, gate.T, filt, skip_gain, kept_blocks.reshape(1, KEPT), out_weight, *constants)


def solution(mesh):
    return jax.shard_map(
        on_device,
        mesh=mesh,
        in_specs=(
            P(("row", "col"), None),
            P("row", "col"),
            P(None, None, None, ("col", "row")),
            P(("col", "row")),
            P(),
            P("col", None),
        ),
        out_specs=P(("row", "col"), None),
        check_vma=False,
    )
```

time: 110 us -> 114 us (1.036)
  Pallas kernels: 104 us -> 108 us
    pallas_call x1, Pallas kernels: 104 us -> 108 us  [on_device(): pl.pallas_call(kernel, out_shape=jax.ShapeDtypeStruct((TOKENS, FEATS), BF...]
where the time goes in v1:
time: 114 us; the launch traced here: 113 us
  Pallas kernels  108 us (95%)
  local copies, waits for them, and re-layouts  5.44 us (5%)
    pallas_call x1, Pallas kernels, on_device(): pl.pallas_call(kernel, out_shape=jax.ShapeDtypeStruct((TOKENS, FEATS), BF...  108 us
    unnamed x2, local copies, waits for them, and re-layouts  5.44 us

profile of v1, /device:TPU:1, one launch (start us, length us, event | category | flops | bytes accessed | tf_op | source)
XLA Modules:
  0.0 113.2 jit_solution(7800793473888574412)
XLA Ops:
  0.0 2.3 %copy.17 = f32[2,256,128,4]{2,1,3,0:T(8,128)} copy(f32[2,256,128,4]{2,3,1,0:T(4,128)} %param.16) | data formatting | bytes 2097152 | tf_op args[2]
  2.3 107.7 %shard_map.136 = bf16[512,2048]{1,0:T(8,128)(2,1)} custom-call(bf16[512,1024]{1,0:T(8,128)(2,1)} %tokens.1, bf16[64,8192]{1,0:T(8,128)(2,1)} %bitcast.6, f32[2,4,256,128]{3,2,1,0:T(8,128)} %bitcast.5, f32[4]{0:T(128)} %skip.1, s32[1,256]{1,0:T(1,128)} %bitcast.7, bf16[64,2048]{1,0:T(8,128)(2,1)} %weight.1, bf16[4,1024,1024]{2,1,0:T(8,128)(2,1)} %constant.16.clone.blocks, ...), custom_call_target="tpu_custom_call" | custom-call | tf_op jit(solution)/shard_map/pallas_call | solution.py:393
  110.0 3.2 %copy.19 = bf16[512,2048]{1,0:T(8,128)(2,1)} copy(bf16[512,2048]{1,0:T(8,128)(2,1)} %shard_map.136) | data formatting | bytes 4194304

commit v2 on v1

--- a/solution.py
+++ b/solution.py
@@ -1,5 +1,3 @@
-import functools
-
 import jax
 import jax.numpy as jnp
 import numpy as np
@@ -203,14 +201,22 @@
         for i, (src, dst) in enumerate(
             [(tokens, tok_v), (pack, pack_v), (blocks, blocks_v), (moves, moves_v), (first, first_v),
              (twist, twist_v), (last, last_v), (edge, edge_v), (mirror, mirror_v),
-             (gate.at[pl.ds(same, 32), :], near_gate), (filt, filt_v)]
+             (gate.at[pl.ds(same, 32), :], near_gate)]
+            + [(filt.at[i, :, c, :], filt_v.at[i, c]) for i in range(2) for c in range(WIDTH)]
         )
     ]
     for load in loads:
         load.start()
-    slice_at = pl.ds(pl.multiple_of((core * 4 + x) * 256, 256), 256)
-    own_weight = pltpu.make_async_copy(weight.at[:, slice_at], w_v.at[zl, y, :, slice_at], own.at[0])
-    own_weight.start()
+
+    def columns(part, width):
+        return pl.ds(pl.multiple_of(core * 1024 + part * 128, 128), width)
+
+    slices = [columns(x, 128), columns(4 + x, 128)]
+    own_weight = [
+        pltpu.make_async_copy(weight.at[:, at], w_v.at[zl, y, :, at], own.at[i]) for i, at in enumerate(slices)
+    ]
+    for load in own_weight:
+        load.start()
 
     loads[0].wait()
     loads[1].wait()
@@ -232,6 +238,10 @@
             device_id=device, device_id_type=MESH,
         )
 
+    for s in range(1, 4):
+        for at in slices:
+            weight_copy(0, weight.at[:, at], w_v.at[zl, y, :, at], (row, lax.rem(zl + s, 4) * 4 + y)).start()
+
     own_tile = pltpu.make_async_copy(sent.at[tile(as_channels)], got.at[tile(as_tokens)], a_recv)
     own_tile.start()
 
@@ -243,10 +253,11 @@
             send_sem=a_send, recv_sem=a_recv, device_id=(to_row, to_col), device_id_type=MESH,
         ).start()
 
-    for s in range(1, 4):
-        weight_copy(
-            0, weight.at[:, slice_at], w_v.at[zl, y, :, slice_at], (row, lax.rem(zl + s, 4) * 4 + y)
-        ).start()
+    def at_x(other):
+        return (zh * 8 + lax.rem(other + 4, 4) * 2 + core, col)
+
+    def at_y(other):
+        return (row, zl * 4 + lax.rem(other + 4, 4))
 
     for load in loads[2:]:
         load.wait()
@@ -255,11 +266,14 @@
     def weight_wait(sem, stage, ref):
         pltpu.make_async_copy(ref, ref, sem.at[stage]).wait()
 
-    own_weight.wait()
-    weight_wait(w_recv, 0, w_v.at[pl.ds(0, 3), 0, :, pl.ds(0, 256)])
+    for load in own_weight:
+        load.wait()
+    weight_wait(w_recv, 0, w_v.at[0, pl.ds(0, 3), :, pl.ds(0, 256)])
     for s in range(1, 4):
-        part = w_v.at[:, y, :, slice_at]
-        weight_copy(1, part, part, (row, zl * 4 + lax.rem(y + s, 4))).start()
+        part = w_v.at[:, y, :, slices[0]]
+        weight_copy(1, part, part, at_y(y + s)).start()
+        part = w_v.at[:, y, :, slices[1]]
+        weight_copy(1, part, part, at_x(x + s)).start()
 
     pltpu.make_async_copy(got, got, a_recv).wait()
 
@@ -278,9 +292,11 @@
         ).start()
 
     weight_wait(w_recv, 1, w_v.at[:, pl.ds(0, 3), :, pl.ds(0, 256)])
-    for s in range(1, 4):
-        part = w_v.at[:, :, :, slice_at]
-        weight_copy(2, part, part, (zh * 8 + lax.rem(x + s, 4) * 2 + core, col)).start()
+    for step in (1, -1):
+        part = w_v.at[:, :, :, slices[0]]
+        weight_copy(2, part, part, at_x(x + step)).start()
+        part = w_v.at[:, y, :, columns(4, 512)]
+        weight_copy(2, part, part, at_y(y + step)).start()
 
     @pl.loop(0, 16)
     def _(g):
@@ -311,6 +327,13 @@
             src_ref=packed.at[row_tiles(to_row)], dst_ref=near.at[row_tiles(low_row)],
             send_sem=n_send, recv_sem=n_recv, device_id=(to_row, col), device_id_type=MESH,
         ).start()
+
+    weight_wait(w_recv, 2, w_v.at[:, :, :, pl.ds(0, 512)])
+    for step, rows in ((1, pl.ds(0, 2)), (-1, pl.ds(2, 2))):
+        part = w_v.at[rows, :, :, columns(lax.rem(x - step + 4, 4), 128)]
+        weight_copy(3, part, part, at_x(x + step)).start()
+        part = w_v.at[rows, lax.rem(y - step + 4, 4), :, columns(4, 512)]
+        weight_copy(3, part, part, at_y(y + step)).start()
 
     @pl.loop(0, 128)
     def _(s):
@@ -345,9 +368,9 @@
             device_id=(row, to_col), device_id_type=MESH,
         ).start()
 
-    weight_wait(w_recv, 2, w_v.at[:, :, :, pl.ds(0, 768)])
-    half = w_v.at[:, :, :, pl.ds(pl.multiple_of(core * 1024, 1024), 1024)]
-    weight_copy(3, half, half, (row + 1 - 2 * core, col)).start()
+    weight_wait(w_recv, 3, w_v.at[:, :, :, pl.ds(0, 256)])
+    half = w_v.at[:, :, :, columns(0, 1024)]
+    weight_copy(4, half, half, (row + 1 - 2 * core, col)).start()
 
     pltpu.make_async_copy(gate_v, gate_v, g_recv).wait()
     pltpu.make_async_copy(returned, returned, b_recv).wait()
@@ -361,7 +384,7 @@
                 piece = rows[i * 128 + h * 32 : i * 128 + h * 32 + 32] * gate_v[g * 2 + i, :, at].astype(F32)
                 gated[g * 2 + i, pl.ds(cross, 32), at] = piece.astype(BF16)
 
-    weight_wait(w_recv, 3, w_v.at[:, :, :, pl.ds(0, 1024)])
+    weight_wait(w_recv, 4, w_v.at[:, :, :, pl.ds(0, 1024)])
     pltpu.make_async_copy(near_out, near_out, m_recv).wait()
 
     @pl.loop(0, 4)
@@ -375,15 +398,16 @@
     pltpu.make_async_copy(gate_v.at[pl.ds(0, 15)], gate_v.at[pl.ds(0, 15)], g_send).wait()
     pltpu.make_async_copy(near.at[pl.ds(0, 1792)], near.at[pl.ds(0, 1792)], n_send).wait()
     pltpu.make_async_copy(near_out.at[pl.ds(0, 15)], near_out.at[pl.ds(0, 15)], m_send).wait()
-    weight_wait(w_send, 0, w_v.at[pl.ds(0, 3), 0, :, pl.ds(0, 256)])
+    weight_wait(w_send, 0, w_v.at[0, pl.ds(0, 3), :, pl.ds(0, 256)])
     weight_wait(w_send, 1, w_v.at[:, pl.ds(0, 3), :, pl.ds(0, 256)])
-    weight_wait(w_send, 2, w_v.at[:, :, :, pl.ds(0, 768)])
-    weight_wait(w_send, 3, w_v.at[:, :, :, pl.ds(0, 1024)])
+    weight_wait(w_send, 2, w_v.at[:, :, :, pl.ds(0, 512)])
+    weight_wait(w_send, 3, w_v.at[:, :, :, pl.ds(0, 256)])
+    weight_wait(w_send, 4, w_v.at[:, :, :, pl.ds(0, 1024)])
 
 
 def on_device(tokens, gate, filter_spectrum, skip_gain, kept_blocks, out_weight):
     constants = [jnp.asarray(t) for t in tables()]
-    filt = jnp.transpose(filter_spectrum, (0, 3, 1, 2))
+    filt = jnp.transpose(filter_spectrum, (0, 1, 3, 2))
     hbm = pl.BlockSpec(memory_space=pl.ANY)
     vmem = pl.BlockSpec(memory_space=pltpu.VMEM)
     smem = pl.BlockSpec(memory_space=pltpu.SMEM)
@@ -392,11 +416,11 @@
     blocks, twist, edge, first, last, pack, moves, mirror = constants
     return pl.pallas_call(
         kernel,
-        out_shape=jax.ShapeDtypeStruct((TOKENS, FEATS), BF16),
+        out_shape=pltpu.VMEM((TOKENS, FEATS), BF16),
         in_specs=[hbm, hbm, hbm, smem, vmem, hbm] + [hbm] * 8,
         out_specs=vmem,
         scratch_shapes=[
-            like(tokens), like(filt), like(blocks), like(twist), like(edge), like(first), like(last), like(pack),
+            like(tokens), pltpu.VMEM((2, WIDTH, KEPT, BLOCK), F32), like(blocks), like(twist), like(edge), like(first), like(last), like(pack),
             like(moves), like(mirror),
             pltpu.VMEM((4096, 128), BF16),
             pltpu.VMEM((4096, 128), BF16),
@@ -418,7 +442,7 @@
             pltpu.VMEM((16, 32, TOKENS), BF16),
             pltpu.VMEM((16, 64, TOKENS), BF16),
             pltpu.VMEM((4, 4, 64, FEATS), BF16),
-            dma((11,)), dma((1,)), dma, dma, dma, dma, dma((4,)), dma((4,)), dma, dma, dma, dma, dma, dma,
+            dma((18,)), dma((2,)), dma, dma, dma, dma, dma((5,)), dma((5,)), dma, dma, dma, dma, dma, dma,
         ],
         compiler_params=pltpu.CompilerParams(
             collective_id=0, has_side_effects=True, vmem_limit_bytes=56 * 1024 * 1024

time: 114 us -> 92.2 us (0.81)
  Pallas kernels: 108 us -> 90.4 us
  local copies, waits for them, and re-layouts: 5.44 us -> 1.32 us
    pallas_call x1, Pallas kernels: 108 us -> 90.4 us  [on_device(): pl.pallas_call(kernel, out_shape=pltpu.VMEM((TOKENS, FEATS), BF16), in_sp...]
    unnamed x2 -> x1, local copies, waits for them, and re-layouts: 5.44 us -> 1.32 us
where the time goes in v2:
time: 92.2 us; the launch traced here: 91.7 us
  Pallas kernels  90.4 us (98%)
  local copies, waits for them, and re-layouts  1.32 us (1%)
    pallas_call x1, Pallas kernels, on_device(): pl.pallas_call(kernel, out_shape=pltpu.VMEM((TOKENS, FEATS), BF16), in_sp...  90.4 us

profile of v2, /device:TPU:1, one launch (start us, length us, event | category | flops | bytes accessed | tf_op | source)
XLA Modules:
  0.0 91.7 jit_solution(3852081888176173664)
XLA Ops:
  0.0 90.4 %shard_map.136 = bf16[512,2048]{1,0:T(8,128)(2,1)S(1)} custom-call(bf16[512,1024]{1,0:T(8,128)(2,1)} %tokens.1, bf16[64,8192]{1,0:T(8,128)(2,1)} %bitcast.3, f32[2,256,4,128]{3,2,1,0:T(4,128)} %bitcast.4, f32[4]{0:T(128)} %skip.1, s32[1,256]{1,0:T(1,128)} %bitcast.5, bf16[64,2048]{1,0:T(8,128)(2,1)} %weight.1, bf16[4,1024,1024]{2,1,0:T(8,128)(2,1)} %constant.16.clone.blocks, ...), custom_call_target="tpu_custom_call" | custom-call | tf_op jit(solution)/shard_map/pallas_call | solution.py:417
  90.4 1.3 %copy.16 = bf16[512,2048]{1,0:T(8,128)(2,1)} copy(bf16[512,2048]{1,0:T(8,128)(2,1)S(1)} %shard_map.136) | data formatting | bytes 4194304

commit v3 on v2

--- a/solution.py
+++ b/solution.py
@@ -187,13 +187,6 @@
     zl, y = col // 4, lax.rem(col, 4)
     as_tokens, as_channels = row * 16 + col, col * 16 + row
 
-    barrier = pltpu.get_barrier_semaphore()
-
-    @pl.loop(1, DEVICES)
-    def _(s):
-        other = (lax.rem(row + s // 16, 16), lax.rem(col + lax.rem(s, 16), 16))
-        pl.semaphore_signal(barrier, inc=1, device_id=other, device_id_type=MESH)
-
     same = pl.multiple_of(zh * 32, 32)
     cross = pl.multiple_of(32 - zh * 32, 32)
     loads = [
@@ -205,8 +198,22 @@
             + [(filt.at[i, :, c, :], filt_v.at[i, c]) for i in range(2) for c in range(WIDTH)]
         )
     ]
-    for load in loads:
+    for load in loads[:2]:
         load.start()
+
+    barrier = pltpu.get_barrier_semaphore()
+
+    columns_on = [lax.rem(col + i, 16) for i in range(16)]
+
+    def greet(to_row, steps):
+        for i in steps:
+            pl.semaphore_signal(barrier, inc=1, device_id=(to_row, columns_on[i]), device_id_type=MESH)
+
+    greet(row, range(1, 16))
+
+    @pl.loop(1, 16)
+    def _(s):
+        greet(lax.rem(row + s, 16), range(16))
 
     def columns(part, width):
         return pl.ds(pl.multiple_of(core * 1024 + part * 128, 128), width)
@@ -245,14 +252,21 @@
     own_tile = pltpu.make_async_copy(sent.at[tile(as_channels)], got.at[tile(as_tokens)], a_recv)
     own_tile.start()
 
-    @pl.loop(1, DEVICES)
-    def _(s):
-        to_row, to_col = lax.rem(row + s // 16, 16), lax.rem(col + lax.rem(s, 16), 16)
-        pltpu.make_async_remote_copy(
-            src_ref=sent.at[tile(to_col * 16 + to_row)], dst_ref=got.at[tile(as_tokens)],
-            send_sem=a_send, recv_sem=a_recv, device_id=(to_row, to_col), device_id_type=MESH,
-        ).start()
-
+    def send_tokens(to_row, steps):
+        for i in steps:
+            pltpu.make_async_remote_copy(
+                src_ref=sent.at[tile(columns_on[i] * 16 + to_row)], dst_ref=got.at[tile(as_tokens)],
+                send_sem=a_send, recv_sem=a_recv, device_id=(to_row, columns_on[i]), device_id_type=MESH,
+            ).start()
+
+    send_tokens(row, range(1, 16))
+
+    @pl.loop(1, 16)
+    def _(s):
+        send_tokens(lax.rem(row + s, 16), range(16))
+
+    for load in loads[2:]:
+        load.start()
     def at_x(other):
         return (zh * 8 + lax.rem(other + 4, 4) * 2 + core, col)
 
@@ -335,14 +349,14 @@
         part = w_v.at[rows, lax.rem(y - step + 4, 4), :, columns(4, 512)]
         weight_copy(3, part, part, at_y(y + step)).start()
 
-    @pl.loop(0, 128)
-    def _(s):
-        to_row = (1 - zh) * 8 + lax.rem(low_row + s // 16, 8)
-        to_col = lax.rem(col + lax.rem(s, 16), 16)
-        pltpu.make_async_remote_copy(
-            src_ref=packed.at[tile(to_row * 16 + to_col)], dst_ref=returned.at[tile(col * 8 + low_row)],
-            send_sem=b_send, recv_sem=b_recv, device_id=(to_row, to_col), device_id_type=MESH,
-        ).start()
+    @pl.loop(0, 8)
+    def _(s):
+        to_row = (1 - zh) * 8 + lax.rem(low_row + s, 8)
+        for to_col in columns_on:
+            pltpu.make_async_remote_copy(
+                src_ref=packed.at[tile(to_row * 16 + to_col)], dst_ref=returned.at[tile(col * 8 + low_row)],
+                send_sem=b_send, recv_sem=b_recv, device_id=(to_row, to_col), device_id_type=MESH,
+            ).start()
 
     pltpu.make_async_copy(near, near, n_recv).wait()
 

time: 92.2 us -> 89.2 us (0.967)
  Pallas kernels: 90.4 us -> 87 us
    pallas_call x1, Pallas kernels: 90.4 us -> 87 us  [on_device(): pl.pallas_call(kernel, out_shape=pltpu.VMEM((TOKENS, FEATS), BF16), in_sp...]
where the time goes in v3:
time: 89.2 us; the launch traced here: 88.3 us
  Pallas kernels  87 us (98%)
  local copies, waits for them, and re-layouts  1.32 us (1%)
    pallas_call x1, Pallas kernels, on_device(): pl.pallas_call(kernel, out_shape=pltpu.VMEM((TOKENS, FEATS), BF16), in_sp...  87 us

profile of v3, /device:TPU:1, one launch (start us, length us, event | category | flops | bytes accessed | tf_op | source)
XLA Modules:
  0.0 88.3 jit_solution(6688171346578382609)
XLA Ops:
  0.0 87.0 %shard_map.136 = bf16[512,2048]{1,0:T(8,128)(2,1)S(1)} custom-call(bf16[512,1024]{1,0:T(8,128)(2,1)} %tokens.1, bf16[64,8192]{1,0:T(8,128)(2,1)} %bitcast.3, f32[2,256,4,128]{3,2,1,0:T(4,128)} %bitcast.4, f32[4]{0:T(128)} %skip.1, s32[1,256]{1,0:T(1,128)} %bitcast.5, bf16[64,2048]{1,0:T(8,128)(2,1)} %weight.1, bf16[4,1024,1024]{2,1,0:T(8,128)(2,1)} %constant.16.clone.blocks, ...), custom_call_target="tpu_custom_call" | custom-call | tf_op jit(solution)/shard_map/pallas_call | solution.py:431
  87.0 1.3 %copy.16 = bf16[512,2048]{1,0:T(8,128)(2,1)} copy(bf16[512,2048]{1,0:T(8,128)(2,1)S(1)} %shard_map.136) | data formatting | bytes 4194304

commit v4 on v3

--- a/solution.py
+++ b/solution.py
@@ -49,6 +49,7 @@
         first[p, 0, :, :, p], first[p, 1, :, :, p] = real, imag
     first = first.reshape(256, 256)
     last = split(first.T.copy())
+    last = np.concatenate([last[0], last[1], last[0]], axis=1)
     first = split(first)
     pack = np.zeros((32, WIDTH, CHUNKS, CHUNKS, 32, WIDTH), np.float32)
     for o in range(32):
@@ -79,6 +80,13 @@
     return lax.dot_general(a, b, (((0,), (0,)), ((), ())), preferred_element_type=F32)
 
 
+def store3(ref, rows, start, width, step, value):
+    high, low = halves(value)
+    ref[rows, start : start + width] = high
+    ref[rows, start + step : start + step + width] = low
+    ref[rows, start + 2 * step : start + 2 * step + width] = high
+
+
 def halves(value):
     high = value.astype(BF16)
     return high, (value - high.astype(F32)).astype(BF16)
@@ -93,37 +101,37 @@
     return [dot(pick, blocks[i]).astype(BF16) for i in range(4)]
 
 
-def prepare(kept, blocks_v, filt_v, mirror_v, tab, filt_p):
+def prepare(kept, blocks_v, filt_v, mirror_v, tab, turned, filt_p):
     cos_high, cos_low, sin_high, sin_low = kept_table(kept[...], blocks_v)
-    tab[0, 0:KEPT, :] = cos_high
-    tab[0, KEPT:, :] = sin_high
-    tab[1, 0:KEPT, :] = cos_low
-    tab[1, KEPT:, :] = sin_low
+    for i, part in enumerate([cos_high, sin_high, cos_high, sin_high, cos_low, sin_low]):
+        tab[i * KEPT : i * KEPT + KEPT, :] = part
+    for i, parts in enumerate([(cos_high, sin_high), (cos_high, sin_high), (cos_low, sin_low)]):
+        for j in range(2):
+            turned[i * BLOCKS : i * BLOCKS + BLOCKS, j * KEPT : j * KEPT + KEPT] = parts[j].T
     for i in range(2):
         for c in range(WIDTH):
             high, low = halves(filt_v[i, c])
             filt_p[i, c] = dot_nt(mirror_v[...], high) + dot_nt(mirror_v[...], low)
 
 
-def convolve(z, first_v, last_v, twist_v, edge_v, tab, filt_p, skip, ends, turn, spec, resp, wave, back, conv):
-    @pl.loop(0, WIDTH)
-    def _(c):
+def convolve(z, first_v, last_v, twist_v, edge_v, tab, turned, filt_p, skip, ends, turn, spec, resp, wave, back, conv):
+    for c in range(WIDTH):
         signal = z[c]
         spread = dot(first_v[0], signal) + dot(first_v[1], signal)
-        rows = pl.ds(pl.multiple_of(c * 128, 128), 128)
+        rows = pl.ds(c * 128, 128)
         for p in range(2):
             at = pl.ds(p * TOKENS, TOKENS)
             re, im = spread[p * 128 : p * 128 + 64], spread[p * 128 + 64 : p * 128 + 128]
             cos, sin, masked = twist_v[0, :, at], twist_v[1, :, at], twist_v[2, :, at]
             both = jnp.concatenate([re * cos + im * sin, im * masked - re * sin], axis=0)
-            turn[0, rows, at], turn[1, rows, at] = halves(both)
+            store3(turn, rows, p * TOKENS, TOKENS, BLOCKS, both)
             ends[pl.ds(c, 1), at] = im[0:1]
 
     edge = ends[0:4, :]
     both = [edge * edge_v[0:1, :], edge * -edge_v[1:2, :], jnp.zeros((8, BLOCKS), F32)]
-    turn[0, 512:528, :], turn[1, 512:528, :] = halves(jnp.concatenate(both, axis=0))
-
-    spec[...] = dot_nt(turn[0], tab[0]) + dot_nt(turn[1], tab[0]) + dot_nt(turn[0], tab[1])
+    store3(turn, pl.ds(512, 16), 0, BLOCKS, BLOCKS, jnp.concatenate(both, axis=0))
+
+    spec[...] = dot(turn[...], turned[...])
 
     top = lax.broadcasted_iota(jnp.int32, (PAIRS, KEPT), 0) == 0
     ends_re, ends_im = [], []
@@ -150,26 +158,27 @@
             ],
             axis=0,
         )
-        resp[0, at : at + 128, :], resp[1, at : at + 128, :] = halves(both)
+        store3(resp, pl.ds(at, 128), 0, 2 * KEPT, 2 * KEPT, both)
     both = jnp.concatenate(ends_re + ends_im + [jnp.zeros((8, 2 * KEPT), F32)], axis=0)
-    resp[0, 512:528, :], resp[1, 512:528, :] = halves(both)
-
-    wave[...] = dot(resp[0], tab[0]) + dot(resp[1], tab[0]) + dot(resp[0], tab[1])
+    store3(resp, pl.ds(512, 16), 0, 2 * KEPT, 2 * KEPT, both)
+
+    wave[...] = dot(resp[...], tab[...])
     edge = wave[512:516, :] * edge_v[0:1, :] - wave[516:520, :] * edge_v[1:2, :]
     ends[0:4, :] = edge
 
-    @pl.loop(0, WIDTH)
-    def _(c):
+    for c in range(WIDTH):
         top = lax.broadcasted_iota(jnp.int32, (PAIRS, TOKENS), 0) == 0
-        start = pl.multiple_of(c * 128, 128)
+        start = c * 128
         for p in range(2):
             at = pl.ds(p * TOKENS, TOKENS)
             re, im = wave[pl.ds(start, 64), at], wave[pl.ds(start + 64, 64), at]
             cos, sin = twist_v[0, :, at], twist_v[1, :, at]
             low = jnp.where(top, ends[pl.ds(c, 1), at], im * cos + re * sin)
             both = jnp.concatenate([re * cos - im * sin, low], axis=0)
-            back[0, p * 128 : p * 128 + 128, :], back[1, p * 128 : p * 128 + 128, :] = halves(both)
-        result = dot(last_v[0], back[0]) + dot(last_v[1], back[0]) + dot(last_v[0], back[1])
+            high, low = halves(both)
+            for i, part in enumerate([high, high, low]):
+                back[c, i * 256 + p * 128 : i * 256 + p * 128 + 128, :] = part
+        result = dot(last_v[...], back[c])
         conv[c] = (result * (1.0 / SEQ) + skip[c] * z[c].astype(F32)).astype(BF16)
 
 
@@ -177,8 +186,8 @@
     tokens, gate, filt, skip, kept, weight, blocks, twist, edge, first, last, pack, moves, mirror,
     out,
     tok_v, filt_v, blocks_v, twist_v, edge_v, first_v, last_v, pack_v, moves_v, mirror_v,
-    sent, got, z, tab, filt_p, ends, turn, spec, resp, wave, back, conv, packed, returned, near, near_gate, near_out,
-    gate_v, gated, w_v,
+    sent, got, z, tab, turned, filt_p, ends, turn, spec, resp, wave, back, conv, packed, returned, near, near_gate, near_out,
+    gate_v, gated, side, w_v,
     local, own, a_send, a_recv, g_send, g_recv, w_send, w_recv, b_send, b_recv, n_send, n_recv, m_send, m_recv,
 ):
     row, col = lax.axis_index("row"), lax.axis_index("col")
@@ -228,11 +237,16 @@
     loads[0].wait()
     loads[1].wait()
 
-    @pl.loop(0, 8)
-    def _(g):
-        at = pl.ds(pl.multiple_of(g * 128, 128), 128)
-        wide = jnp.concatenate([tok_v[pl.ds(h * 128, 128), at] for h in range(CHUNKS)], axis=1)
-        sent[pl.ds(pl.multiple_of(g * 512, 512), 512), :] = dot_nt(pack_v[...], wide).astype(BF16)
+    @pl.loop(0, 2)
+    def _(part):
+        wide = []
+        for i in range(4):
+            at = pl.ds(pl.multiple_of((part * 4 + i) * 128, 128), 128)
+            wide.append(jnp.concatenate([tok_v[pl.ds(h * 128, 128), at] for h in range(CHUNKS)], axis=1))
+        rows = [dot_nt(pack_v[...], jnp.concatenate(wide[i : i + 2], axis=0)).astype(BF16) for i in (0, 2)]
+        for i in range(4):
+            at = pl.ds(pl.multiple_of((part * 4 + i) * 512, 512), 512)
+            sent[at, :] = rows[i // 2][:, i % 2 * 128 : i % 2 * 128 + 128]
 
     pl.semaphore_wait(barrier, DEVICES - 1)
 
@@ -275,7 +289,7 @@
 
     for load in loads[2:]:
         load.wait()
-    prepare(kept, blocks_v, filt_v, mirror_v, tab, filt_p)
+    prepare(kept, blocks_v, filt_v, mirror_v, tab, turned, filt_p)
 
     def weight_wait(sem, stage, ref):
         pltpu.make_async_copy(ref, ref, sem.at[stage]).wait()
@@ -312,21 +326,35 @@
         part = w_v.at[:, y, :, columns(4, 512)]
         weight_copy(2, part, part, at_y(y + step)).start()
 
-    @pl.loop(0, 16)
-    def _(g):
-        rows = dot(moves_v[0], got[pl.ds(pl.multiple_of(g * 256, 256), 256), :]).astype(BF16)
-        for c in range(WIDTH):
-            for h in range(CHUNKS):
-                z[c, tile(g), pl.ds(h * 128, 128)] = rows[(c * 4 + h) * 16 : (c * 4 + h) * 16 + 16, :]
-
-    convolve(z, first_v, last_v, twist_v, edge_v, tab, filt_p, skip, ends, turn, spec, resp, wave, back, conv)
-
-    @pl.loop(0, 16)
-    def _(g):
-        rows = jnp.concatenate(
-            [conv[c, tile(g), pl.ds(h * 128, 128)] for c in range(WIDTH) for h in range(CHUNKS)], axis=0
-        )
-        packed[pl.ds(pl.multiple_of(g * 256, 256), 256), :] = dot(moves_v[1], rows).astype(BF16)
+    def group(ref, g):
+        return ref[pl.ds(pl.multiple_of(g * 256, 256), 256), :]
+
+    def moved(which, pieces):
+        rows = [dot(moves_v[which], jnp.concatenate(pieces[i : i + 2], axis=1)) for i in range(0, len(pieces), 2)]
+        return [half for pair in rows for half in (pair[:, :128], pair[:, 128:])]
+
+    @pl.loop(0, 4)
+    def _(part):
+        rows = moved(0, [group(got, part * 4 + i) for i in range(4)])
+        for i in range(4):
+            piece = rows[i].astype(BF16)
+            for c in range(WIDTH):
+                for h in range(CHUNKS):
+                    at = (c * 4 + h) * 16
+                    z[c, tile(part * 4 + i), pl.ds(h * 128, 128)] = piece[at : at + 16, :]
+
+    convolve(z, first_v, last_v, twist_v, edge_v, tab, turned, filt_p, skip, ends, turn, spec, resp, wave, back, conv)
+
+    @pl.loop(0, 4)
+    def _(part):
+        pieces = []
+        for i in range(4):
+            at = tile(part * 4 + i)
+            rows = [conv[c, at, pl.ds(h * 128, 128)] for c in range(WIDTH) for h in range(CHUNKS)]
+            pieces.append(jnp.concatenate(rows, axis=0))
+        rows = moved(1, pieces)
+        for i in range(4):
+            packed[pl.ds(pl.multiple_of((part * 4 + i) * 256, 256), 256), :] = rows[i].astype(BF16)
 
     def row_tiles(index):
         return pl.ds(pl.multiple_of(index * 256, 256), 256)
@@ -341,13 +369,6 @@
             src_ref=packed.at[row_tiles(to_row)], dst_ref=near.at[row_tiles(low_row)],
             send_sem=n_send, recv_sem=n_recv, device_id=(to_row, col), device_id_type=MESH,
         ).start()
-
-    weight_wait(w_recv, 2, w_v.at[:, :, :, pl.ds(0, 512)])
-    for step, rows in ((1, pl.ds(0, 2)), (-1, pl.ds(2, 2))):
-        part = w_v.at[rows, :, :, columns(lax.rem(x - step + 4, 4), 128)]
-        weight_copy(3, part, part, at_x(x + step)).start()
-        part = w_v.at[rows, lax.rem(y - step + 4, 4), :, columns(4, 512)]
-        weight_copy(3, part, part, at_y(y + step)).start()
 
     @pl.loop(0, 8)
     def _(s):
@@ -358,17 +379,29 @@
                 send_sem=b_send, recv_sem=b_recv, device_id=(to_row, to_col), device_id_type=MESH,
             ).start()
 
+    weight_wait(w_recv, 2, w_v.at[:, :, :, pl.ds(0, 512)])
+    for step, rows in ((1, pl.ds(0, 2)), (-1, pl.ds(2, 2))):
+        part = w_v.at[rows, :, :, columns(lax.rem(x - step + 4, 4), 128)]
+        weight_copy(3, part, part, at_x(x + step)).start()
+        part = w_v.at[rows, lax.rem(y - step + 4, 4), :, columns(4, 512)]
+        weight_copy(3, part, part, at_y(y + step)).start()
+
     pltpu.make_async_copy(near, near, n_recv).wait()
 
-    @pl.loop(0, 8)
-    def _(g):
-        rows = jnp.concatenate([near[tile(s * 16 + g * 2 + i), :] for i in range(2) for s in range(8)], axis=0)
-        rows = dot(moves_v[2], rows)
-        for i in range(2):
+    @pl.loop(0, 2)
+    def _(part):
+        pieces = []
+        for n in range(4):
+            at = part * 8 + n * 2
+            rows = [near[tile(s * 16 + at + i), :] for i in range(2) for s in range(8)]
+            pieces.append(jnp.concatenate(rows, axis=0))
+        rows = moved(2, pieces)
+        for n in range(8):
             for h in range(CHUNKS):
-                at = pl.ds(pl.multiple_of((g * 2 + i) * TOKENS + h * 128, 128), 128)
-                piece = rows[i * 128 + h * 32 : i * 128 + h * 32 + 32] * near_gate[:, at].astype(F32)
-                near_out[g * 2 + i, :, pl.ds(h * 128, 128)] = piece.astype(BF16)
+                at = pl.ds(pl.multiple_of((part * 8 + n) * TOKENS + h * 128, 128), 128)
+                from_row = n % 2 * 128 + h * 32
+                piece = rows[n // 2][from_row : from_row + 32] * near_gate[:, at].astype(F32)
+                near_out[part * 8 + n, :, pl.ds(h * 128, 128)] = piece.astype(BF16)
 
     mine = gated.at[col, pl.ds(same, 32), :]
     own_out = pltpu.make_async_copy(near_out.at[col], mine, m_recv)
@@ -389,23 +422,25 @@
     pltpu.make_async_copy(gate_v, gate_v, g_recv).wait()
     pltpu.make_async_copy(returned, returned, b_recv).wait()
 
-    @pl.loop(0, 8)
-    def _(g):
-        rows = dot(moves_v[2], returned[pl.ds(pl.multiple_of(g * 256, 256), 256), :])
-        for i in range(2):
+    @pl.loop(0, 2)
+    def _(part):
+        rows = moved(2, [group(returned, part * 4 + i) for i in range(4)])
+        for n in range(8):
             for h in range(CHUNKS):
                 at = pl.ds(h * 128, 128)
-                piece = rows[i * 128 + h * 32 : i * 128 + h * 32 + 32] * gate_v[g * 2 + i, :, at].astype(F32)
-                gated[g * 2 + i, pl.ds(cross, 32), at] = piece.astype(BF16)
+                from_row = n % 2 * 128 + h * 32
+                piece = rows[n // 2][from_row : from_row + 32] * gate_v[part * 8 + n, :, at].astype(F32)
+                gated[part * 8 + n, pl.ds(cross, 32), at] = piece.astype(BF16)
 
     weight_wait(w_recv, 4, w_v.at[:, :, :, pl.ds(0, 1024)])
     pltpu.make_async_copy(near_out, near_out, m_recv).wait()
+
+    side[...] = gated[...].reshape(1024, TOKENS).T
 
     @pl.loop(0, 4)
     def _(n):
         at = pl.ds(pl.multiple_of(n * 512, 512), 512)
-        left = gated[...].reshape(1024, TOKENS)
-        out[:, at] = dot_tn(left, w_v[:, :, :, at].reshape(1024, 512)).astype(BF16)
+        out[:, at] = dot(side[...], w_v[:, :, :, at].reshape(1024, 512)).astype(BF16)
 
     pltpu.make_async_copy(sent.at[pl.ds(0, 4080)], sent.at[pl.ds(0, 4080)], a_send).wait()
     pltpu.make_async_copy(returned, returned, b_send).wait()
@@ -439,14 +474,15 @@
             pltpu.VMEM((4096, 128), BF16),
             pltpu.VMEM((4096, 128), BF16),
             pltpu.VMEM((WIDTH, 256, TOKENS), BF16),
-            pltpu.VMEM((2, 2 * KEPT, BLOCKS), BF16),
+            pltpu.VMEM((6 * KEPT, BLOCKS), BF16),
+            pltpu.VMEM((3 * BLOCKS, 2 * KEPT), BF16),
             pltpu.VMEM((2, WIDTH, BLOCK, KEPT), F32),
             pltpu.VMEM((8, BLOCKS), F32),
-            pltpu.VMEM((2, 528, BLOCKS), BF16),
+            pltpu.VMEM((528, 3 * BLOCKS), BF16),
             pltpu.VMEM((528, 2 * KEPT), F32),
-            pltpu.VMEM((2, 528, 2 * KEPT), BF16),
+            pltpu.VMEM((528, 6 * KEPT), BF16),
             pltpu.VMEM((528, BLOCKS), F32),
-            pltpu.VMEM((2, 256, TOKENS), BF16),
+            pltpu.VMEM((WIDTH, 768, TOKENS), BF16),
             pltpu.VMEM((WIDTH, 256, TOKENS), BF16),
             pltpu.VMEM((4096, 128), BF16),
             pltpu.VMEM((2048, 128), BF16),
@@ -455,6 +491,7 @@
             pltpu.VMEM((16, 32, TOKENS), BF16),
             pltpu.VMEM((16, 32, TOKENS), BF16),
             pltpu.VMEM((16, 64, TOKENS), BF16),
+            pltpu.VMEM((TOKENS, 1024), BF16),
             pltpu.VMEM((4, 4, 64, FEATS), BF16),
             dma((18,)), dma((2,)), dma, dma, dma, dma, dma((5,)), dma((5,)), dma, dma, dma, dma, dma, dma,
         ],

time: 89.2 us -> 83.7 us (0.938)
  Pallas kernels: 87 us -> 81.2 us
    pallas_call x1, Pallas kernels: 87 us -> 81.2 us  [on_device(): pl.pallas_call(kernel, out_shape=pltpu.VMEM((TOKENS, FEATS), BF16), in_sp...]
where the time goes in v4:
time: 83.7 us; the launch traced here: 82.6 us
  Pallas kernels  81.2 us (97%)
  local copies, waits for them, and re-layouts  1.32 us (2%)
    pallas_call x1, Pallas kernels, on_device(): pl.pallas_call(kernel, out_shape=pltpu.VMEM((TOKENS, FEATS), BF16), in_sp...  81.2 us

profile of v4, /device:TPU:1, one launch (start us, length us, event | category | flops | bytes accessed | tf_op | source)
XLA Modules:
  0.0 82.6 jit_solution(13196731295306338782)
XLA Ops:
  0.0 81.2 %shard_map.136 = bf16[512,2048]{1,0:T(8,128)(2,1)S(1)} custom-call(bf16[512,1024]{1,0:T(8,128)(2,1)} %tokens.1, bf16[64,8192]{1,0:T(8,128)(2,1)} %bitcast.3, f32[2,256,4,128]{3,2,1,0:T(4,128)} %bitcast.4, f32[4]{0:T(128)} %skip.1, s32[1,256]{1,0:T(1,128)} %bitcast.5, bf16[64,2048]{1,0:T(8,128)(2,1)} %weight.1, bf16[4,1024,1024]{2,1,0:T(8,128)(2,1)} %constant.16.clone.blocks, ...), custom_call_target="tpu_custom_call" | custom-call | tf_op jit(solution)/shard_map/pallas_call | solution.py:466
  81.2 1.3 %copy.16 = bf16[512,2048]{1,0:T(8,128)(2,1)} copy(bf16[512,2048]{1,0:T(8,128)(2,1)S(1)} %shard_map.136) | data formatting | bytes 4194304

commit v5 on v4

--- a/solution.py
+++ b/solution.py
@@ -187,7 +187,7 @@
     out,
     tok_v, filt_v, blocks_v, twist_v, edge_v, first_v, last_v, pack_v, moves_v, mirror_v,
     sent, got, z, tab, turned, filt_p, ends, turn, spec, resp, wave, back, conv, packed, returned, near, near_gate, near_out,
-    gate_v, gated, side, w_v,
+    gate_v, gated_near, gated_far, side, total, w_v,
     local, own, a_send, a_recv, g_send, g_recv, w_send, w_recv, b_send, b_recv, n_send, n_recv, m_send, m_recv,
 ):
     row, col = lax.axis_index("row"), lax.axis_index("col")
@@ -305,6 +305,10 @@
 
     pltpu.make_async_copy(got, got, a_recv).wait()
 
+    def far_column(s):
+        ahead = lax.rem(col + s - 1 + s // 9, 8)
+        return lax.rem(col // 8 + 1 + s // 9, 2) * 8 + ahead
+
     def gate_at(to_col):
         return gate.at[pl.ds(cross, 32), pl.ds(pl.multiple_of(to_col * TOKENS, TOKENS), TOKENS)]
 
@@ -313,7 +317,7 @@
 
     @pl.loop(1, 16)
     def _(s):
-        to_col = lax.rem(col + s, 16)
+        to_col = far_column(s)
         pltpu.make_async_remote_copy(
             src_ref=gate_at(to_col), dst_ref=gate_v.at[col], send_sem=g_send, recv_sem=g_recv,
             device_id=(row, to_col), device_id_type=MESH,
@@ -362,15 +366,29 @@
     own_near = pltpu.make_async_copy(packed.at[row_tiles(row)], near.at[row_tiles(low_row)], n_recv)
     own_near.start()
 
-    @pl.loop(1, 8)
+    def send_near():
+        @pl.loop(1, 8)
+        def _(s):
+            to_row = zh * 8 + lax.rem(low_row + s, 8)
+            pltpu.make_async_remote_copy(
+                src_ref=packed.at[row_tiles(to_row)], dst_ref=near.at[row_tiles(low_row)],
+                send_sem=n_send, recv_sem=n_recv, device_id=(to_row, col), device_id_type=MESH,
+            ).start()
+
+    pl.when(zh == 0)(send_near)
+
+    @pl.loop(0, 3)
     def _(s):
-        to_row = zh * 8 + lax.rem(low_row + s, 8)
-        pltpu.make_async_remote_copy(
-            src_ref=packed.at[row_tiles(to_row)], dst_ref=near.at[row_tiles(low_row)],
-            send_sem=n_send, recv_sem=n_recv, device_id=(to_row, col), device_id_type=MESH,
-        ).start()
-
-    @pl.loop(0, 8)
+        to_row = (1 - zh) * 8 + lax.rem(low_row + s, 8)
+        for to_col in columns_on:
+            pltpu.make_async_remote_copy(
+                src_ref=packed.at[tile(to_row * 16 + to_col)], dst_ref=returned.at[tile(col * 8 + low_row)],
+                send_sem=b_send, recv_sem=b_recv, device_id=(to_row, to_col), device_id_type=MESH,
+            ).start()
+
+    pl.when(zh == 1)(send_near)
+
+    @pl.loop(3, 8)
     def _(s):
         to_row = (1 - zh) * 8 + lax.rem(low_row + s, 8)
         for to_col in columns_on:
@@ -403,13 +421,13 @@
                 piece = rows[n // 2][from_row : from_row + 32] * near_gate[:, at].astype(F32)
                 near_out[part * 8 + n, :, pl.ds(h * 128, 128)] = piece.astype(BF16)
 
-    mine = gated.at[col, pl.ds(same, 32), :]
+    mine = gated_near.at[col]
     own_out = pltpu.make_async_copy(near_out.at[col], mine, m_recv)
     own_out.start()
 
     @pl.loop(1, 16)
     def _(s):
-        to_col = lax.rem(col + s, 16)
+        to_col = far_column(s)
         pltpu.make_async_remote_copy(
             src_ref=near_out.at[to_col], dst_ref=mine, send_sem=m_send, recv_sem=m_recv,
             device_id=(row, to_col), device_id_type=MESH,
@@ -430,17 +448,27 @@
                 at = pl.ds(h * 128, 128)
                 from_row = n % 2 * 128 + h * 32
                 piece = rows[n // 2][from_row : from_row + 32] * gate_v[part * 8 + n, :, at].astype(F32)
-                gated[part * 8 + n, pl.ds(cross, 32), at] = piece.astype(BF16)
+                gated_far[part * 8 + n, :, at] = piece.astype(BF16)
 
     weight_wait(w_recv, 4, w_v.at[:, :, :, pl.ds(0, 1024)])
-    pltpu.make_async_copy(near_out, near_out, m_recv).wait()
-
-    side[...] = gated[...].reshape(1024, TOKENS).T
+
+    def project(start, at):
+        return dot(side[...], w_v[:, :, pl.ds(start, 32), at].reshape(512, 512))
+
+    side[...] = gated_far[...].reshape(512, TOKENS).T
 
     @pl.loop(0, 4)
     def _(n):
         at = pl.ds(pl.multiple_of(n * 512, 512), 512)
-        out[:, at] = dot(side[...], w_v[:, :, :, at].reshape(1024, 512)).astype(BF16)
+        total[:, at] = project(cross, at)
+
+    pltpu.make_async_copy(near_out, near_out, m_recv).wait()
+    side[...] = gated_near[...].reshape(512, TOKENS).T
+
+    @pl.loop(0, 4)
+    def _(n):
+        at = pl.ds(pl.multiple_of(n * 512, 512), 512)
+        out[:, at] = (total[:, at] + project(same, at)).astype(BF16)
 
     pltpu.make_async_copy(sent.at[pl.ds(0, 4080)], sent.at[pl.ds(0, 4080)], a_send).wait()
     pltpu.make_async_copy(returned, returned, b_send).wait()
@@ -490,8 +518,10 @@
             pltpu.VMEM((32, 16 * TOKENS), BF16),
             pltpu.VMEM((16, 32, TOKENS), BF16),
             pltpu.VMEM((16, 32, TOKENS), BF16),
-            pltpu.VMEM((16, 64, TOKENS), BF16),
-            pltpu.VMEM((TOKENS, 1024), BF16),
+            pltpu.VMEM((16, 32, TOKENS), BF16),
+            pltpu.VMEM((16, 32, TOKENS), BF16),
+            pltpu.VMEM((TOKENS, 512), BF16),
+            pltpu.VMEM((TOKENS, FEATS), F32),
             pltpu.VMEM((4, 4, 64, FEATS), BF16),
             dma((18,)), dma((2,)), dma, dma, dma, dma, dma((5,)), dma((5,)), dma, dma, dma, dma, dma, dma,
         ],

time: 83.7 us -> 83.2 us (level)
  no operation moved by 1% of the time
where the time goes in v5:
time: 83.2 us; the launch traced here: 82.7 us
  Pallas kernels  81.3 us (98%)
  local copies, waits for them, and re-layouts  1.32 us (2%)
    pallas_call x1, Pallas kernels, on_device(): pl.pallas_call(kernel, out_shape=pltpu.VMEM((TOKENS, FEATS), BF16), in_sp...  81.3 us

profile of v5, /device:TPU:1, one launch (start us, length us, event | category | flops | bytes accessed | tf_op | source)
XLA Modules:
  0.0 82.7 jit_solution(14033330906889163896)
XLA Ops:
  0.0 81.3 %shard_map.136 = bf16[512,2048]{1,0:T(8,128)(2,1)S(1)} custom-call(bf16[512,1024]{1,0:T(8,128)(2,1)} %tokens.1, bf16[64,8192]{1,0:T(8,128)(2,1)} %bitcast.3, f32[2,256,4,128]{3,2,1,0:T(4,128)} %bitcast.4, f32[4]{0:T(128)} %skip.1, s32[1,256]{1,0:T(1,128)} %bitcast.5, bf16[64,2048]{1,0:T(8,128)(2,1)} %weight.1, bf16[4,1024,1024]{2,1,0:T(8,128)(2,1)} %constant.16.clone.blocks, ...), custom_call_target="tpu_custom_call" | custom-call | tf_op jit(solution)/shard_map/pallas_call | solution.py:494
  81.3 1.3 %copy.16 = bf16[512,2048]{1,0:T(8,128)(2,1)} copy(bf16[512,2048]{1,0:T(8,128)(2,1)S(1)} %shard_map.136) | data formatting | bytes 4194304

commit v6 on v5

--- a/solution.py
+++ b/solution.py
@@ -349,8 +349,7 @@
 
     convolve(z, first_v, last_v, twist_v, edge_v, tab, turned, filt_p, skip, ends, turn, spec, resp, wave, back, conv)
 
-    @pl.loop(0, 4)
-    def _(part):
+    def pack_rows(part):
         pieces = []
         for i in range(4):
             at = tile(part * 4 + i)
@@ -360,11 +359,10 @@
         for i in range(4):
             packed[pl.ds(pl.multiple_of((part * 4 + i) * 256, 256), 256), :] = rows[i].astype(BF16)
 
+    pl.loop(0, 2)(pack_rows)
+
     def row_tiles(index):
         return pl.ds(pl.multiple_of(index * 256, 256), 256)
-
-    own_near = pltpu.make_async_copy(packed.at[row_tiles(row)], near.at[row_tiles(low_row)], n_recv)
-    own_near.start()
 
     def send_near():
         @pl.loop(1, 8)
@@ -375,10 +373,7 @@
                 send_sem=n_send, recv_sem=n_recv, device_id=(to_row, col), device_id_type=MESH,
             ).start()
 
-    pl.when(zh == 0)(send_near)
-
-    @pl.loop(0, 3)
-    def _(s):
+    def send_far(s):
         to_row = (1 - zh) * 8 + lax.rem(low_row + s, 8)
         for to_col in columns_on:
             pltpu.make_async_remote_copy(
@@ -386,16 +381,24 @@
                 send_sem=b_send, recv_sem=b_recv, device_id=(to_row, to_col), device_id_type=MESH,
             ).start()
 
+    pl.when(zh == 0)(send_near)
+
+    @pl.when(zh == 1)
+    def _():
+        pl.loop(0, 3)(send_far)
+
+    pl.loop(2, 4)(pack_rows)
+
+    own_near = pltpu.make_async_copy(packed.at[row_tiles(row)], near.at[row_tiles(low_row)], n_recv)
+    own_near.start()
+
+    @pl.when(zh == 0)
+    def _():
+        pl.loop(0, 3)(send_far)
+
     pl.when(zh == 1)(send_near)
 
-    @pl.loop(3, 8)
-    def _(s):
-        to_row = (1 - zh) * 8 + lax.rem(low_row + s, 8)
-        for to_col in columns_on:
-            pltpu.make_async_remote_copy(
-                src_ref=packed.at[tile(to_row * 16 + to_col)], dst_ref=returned.at[tile(col * 8 + low_row)],
-                send_sem=b_send, recv_sem=b_recv, device_id=(to_row, to_col), device_id_type=MESH,
-            ).start()
+    pl.loop(3, 8)(send_far)
 
     weight_wait(w_recv, 2, w_v.at[:, :, :, pl.ds(0, 512)])
     for step, rows in ((1, pl.ds(0, 2)), (-1, pl.ds(2, 2))):

time: 83.2 us -> 83.8 us (level)
  Pallas kernels: 81.3 us -> 82.4 us
    pallas_call x1, Pallas kernels: 81.3 us -> 82.4 us  [on_device(): pl.pallas_call(kernel, out_shape=pltpu.VMEM((TOKENS, FEATS), BF16), in_sp...]
where the time goes in v6:
time: 83.8 us; the launch traced here: 83.7 us
  Pallas kernels  82.4 us (98%)
  local copies, waits for them, and re-layouts  1.32 us (2%)
    pallas_call x1, Pallas kernels, on_device(): pl.pallas_call(kernel, out_shape=pltpu.VMEM((TOKENS, FEATS), BF16), in_sp...  82.4 us

profile of v6, /device:TPU:1, one launch (start us, length us, event | category | flops | bytes accessed | tf_op | source)
XLA Modules:
  0.0 83.7 jit_solution(2268410309269312383)
XLA Ops:
  0.0 82.4 %shard_map.136 = bf16[512,2048]{1,0:T(8,128)(2,1)S(1)} custom-call(bf16[512,1024]{1,0:T(8,128)(2,1)} %tokens.1, bf16[64,8192]{1,0:T(8,128)(2,1)} %bitcast.3, f32[2,256,4,128]{3,2,1,0:T(4,128)} %bitcast.4, f32[4]{0:T(128)} %skip.1, s32[1,256]{1,0:T(1,128)} %bitcast.5, bf16[64,2048]{1,0:T(8,128)(2,1)} %weight.1, bf16[4,1024,1024]{2,1,0:T(8,128)(2,1)} %constant.16.clone.blocks, ...), custom_call_target="tpu_custom_call" | custom-call | tf_op jit(solution)/shard_map/pallas_call | solution.py:497
  82.4 1.3 %copy.16 = bf16[512,2048]{1,0:T(8,128)(2,1)} copy(bf16[512,2048]{1,0:T(8,128)(2,1)S(1)} %shard_map.136) | data formatting | bytes 4194304
